TPU v7x, 32 devices: a whole 2x2x4 slice. The times are simulated.
32 devices in a mesh: film: 2 (over y), tm: 4 (over z), rows: 2 (over x), cols: 2 (over core).
Axes of the slice: x: 2, y: 2, z: 4, core: 2. Of those that a mesh axis runs over, the one named last changes fastest.
Arguments:
- noisy_luma: float32 [32, 256, 1536], P(('film', 'tm'), 'rows', 'cols'), parts along dimension 0, may hold values from -6 to 6
- scene_cuts: int32 [6], P('film'), parts along dimension 0, may hold values from 1 to 15
Outputs:
- denoised: float32 [32, 256, 1536], P(('film', 'tm'), 'rows', 'cols'), parts along dimension 0
There are 2 independent parts, one for each index of `film`. A program takes and returns all parts, laid end to end along the dimension named above; each array names one. Nothing has to cross between parts.
All inputs are finite; a program needn't handle non-finite values.
Results may differ from a plain program's by a relative error of at most 0.00002.
Values sent between devices are 32-bit elements; how exact they have to be, the bound alone decides.
A program may use at most 64 MiB of HBM per device.

v0:
```python
import jax
import jax.numpy as jnp
from jax import lax
from jax.sharding import PartitionSpec as P

ITERS = 4


dual_step = 12.0 ** (-0.5)
primal_step = 12.0 ** (-0.5)
radius = 0.6


def from_behind(value, axis, steps):
    count = lax.axis_size(axis)
    initial, last = (max(0, -steps), min(count, count - steps))
    return lax.ppermute(value, axis, [(source, source + steps) for source in range(initial, last)])


def make_masks(scene_cuts, offset, length, extent, temporal):
    indices = offset + jnp.arange(length, dtype=jnp.int32)
    inside = (indices >= 0) & (indices <= extent - 2)
    if temporal:
        struck = jnp.any(scene_cuts[None, :] == indices[:, None] + 1, axis=1)
        inside = inside & jnp.logical_not(struck)
    return inside.astype(jnp.float32)


def project(dual_parts, slopes):
    stepped = [previous + dual_step * slope for previous, slope in zip(dual_parts, slopes)]
    magnitude = jnp.sqrt(
        stepped[0] * stepped[0] + stepped[1] * stepped[1] + stepped[2] * stepped[2]
    )
    shrink = 1.0 / jnp.maximum(1.0, magnitude / radius)
    return (stepped[0] * shrink, stepped[1] * shrink, stepped[2] * shrink)


def primal_update(current, diverged, noisy_luma):
    return (current + primal_step * diverged + primal_step * noisy_luma) / (1.0 + primal_step)


def forward_faces(values, mask_t, mask_h, mask_w):
    after_t = from_behind(values[:1], "tm", -1)
    after_h = from_behind(values[:, :1], "rows", -1)
    after_w = from_behind(values[:, :, :1], "cols", -1)
    slope_t = (jnp.concatenate([values[1:], after_t], 0) - values) * mask_t[:, None, None]
    slope_h = (jnp.concatenate([values[:, 1:], after_h], 1) - values) * mask_h[None, :, None]
    slope_w = (jnp.concatenate([values[:, :, 1:], after_w], 2) - values) * mask_w[None, None, :]
    return (slope_t, slope_h, slope_w)


def backward_faces(dual_t, dual_h, dual_w):
    before_t = from_behind(dual_t[-1:], "tm", 1)
    before_h = from_behind(dual_h[:, -1:], "rows", 1)
    before_w = from_behind(dual_w[:, :, -1:], "cols", 1)
    return (
        dual_t
        - jnp.concatenate([before_t, dual_t[:-1]], 0)
        + (dual_h - jnp.concatenate([before_h, dual_h[:, :-1]], 1))
        + (dual_w - jnp.concatenate([before_w, dual_w[:, :, :-1]], 2))
    )


def body(noisy_luma, scene_cuts):
    frames_dev, rows_dev, cols_dev = noisy_luma.shape
    frames_all = frames_dev * lax.axis_size("tm")
    rows_all = rows_dev * lax.axis_size("rows")
    cols_all = cols_dev * lax.axis_size("cols")
    first_frame = lax.axis_index("tm") * frames_dev
    first_row = lax.axis_index("rows") * rows_dev
    first_col = lax.axis_index("cols") * cols_dev
    mask_t = make_masks(scene_cuts, first_frame, frames_dev, frames_all, True)
    mask_h = make_masks(scene_cuts, first_row, rows_dev, rows_all, False)
    mask_w = make_masks(scene_cuts, first_col, cols_dev, cols_all, False)
    current = noisy_luma
    relaxed = noisy_luma
    zeroes = jnp.zeros_like(noisy_luma)
    dual_parts = (zeroes, zeroes, zeroes)
    for sweep in range(ITERS):
        slopes = forward_faces(relaxed, mask_t, mask_h, mask_w)
        dual_parts = project(dual_parts, slopes)
        diverged = backward_faces(dual_parts[0], dual_parts[1], dual_parts[2])
        updated = primal_update(current, diverged, noisy_luma)
        relaxed = 2.0 * updated - current
        current = updated
    return current


def solution(mesh):
    return jax.shard_map(
        body,
        mesh=mesh,
        in_specs=(P(("film", "tm"), "rows", "cols"), P("film")),
        out_specs=P(("film", "tm"), "rows", "cols"),
        check_vma=False,
    )
```

profile of v0, /device:TPU:0, one launch (start us, length us, event | category | flops | bytes accessed | tf_op | source)
XLA Modules:
  0.0 118.3 jit_solution(7757432457373596911)
XLA Ops:
  3.2 1.4 %collective-permute-start.2 = (f32[4,128,1]{2,1,0:T(8,128)S(1)}, f32[4,128,1]{2,1,0:T(8,128)S(1)}, u32[]{:S(2)}, u32[]{:S(2)}) collective-permute-start(f32[4,128,1]{2,1,0:T(8,128)S(1)} %slice.149), channel_id=1, source_target_pairs={{1,0},{3,2},{5,4},{7,6},{9,8},{11,10},{13,12},{15,14},{17,16},{19,... | collective-permute-start | bytes 6152 | tf_op jit(solution)/shard_map/ppermute | solution.py:17
  7.8 1.4 %slice.144 = f32[3,128,768]{2,1,0:T(8,128)S(1)} slice(f32[4,128,768]{2,1,0:T(8,128)} %param.2), slice={[1:4], [0:128], [0:768]} | slice | bytes 2359296 | tf_op jit(solution)/shard_map/slice | solution.py:46
  9.8 10.3 %collective-permute-done = f32[1,128,768]{2,1,0:T(8,128)S(1)} collective-permute-done((f32[1,128,768]{2,1,0:T(8,128)S(1)}, f32[1,128,768]{2,1,0:T(8,128)S(1)}, u32[]{:S(2)}, u32[]{:S(2)}) %collective-permute-start) | collective-permute-done | bytes 393248 | tf_op jit(solution)/shard_map/ppermute | solution.py:17
  20.2 1.4 %fusion.54 = (f32[4,128,768]{2,1,0:T(8,128)S(1)}, f32[4,128,768]{2,1,0:T(8,128)S(1)}) fusion(f32[768]{0:T(1024)S(1)} %fusion.58, f32[4,128,768]{2,1,0:T(8,128)S(1)} %copy-done, f32[4,128,1]{2,1,0:T(8,128)S(1)} %collective-permute-done.2, f32[4,128,767]{2,1,0:T(8,128)S(1)} %slice.148, f32[128]{0:T(128)S(1)} %and_convert_fusion, ...), kind=kLoop, calls=%fused_computation.85 | loop fusion | flops 8257536 | bytes 9440784 | tf_op jit(solution)/shard_map/mul | solution.py:35
  22.1 4.1 %collective-permute-start.3 = (f32[1,128,768]{2,1,0:T(8,128)S(1)}, f32[1,128,768]{2,1,0:T(8,128)S(1)}, u32[]{:S(2)}, u32[]{:S(2)}) collective-permute-start(f32[1,128,768]{2,1,0:T(8,128)S(1)} %slice.192), channel_id=1, source_target_pairs={{0,4},{4,8},{8,12},{1,5},{5,9},{9,13},{2,6},{6,10},{10,14},{3,7},{... | collective-permute-start | bytes 1179656 | tf_op jit(solution)/shard_map/ppermute | solution.py:17
  26.3 4.5 %collective-permute-start.4 = (f32[4,1,768]{2,1,0:T(1,128)S(1)}, f32[4,1,768]{2,1,0:T(1,128)S(1)}, u32[]{:S(2)}, u32[]{:S(2)}) collective-permute-start(f32[4,1,768]{2,1,0:T(1,128)S(1)} %slice.194), channel_id=1, source_target_pairs={{0,2},{1,3},{4,6},{5,7},{8,10},{9,11},{12,14},{13,15},{16,18},{17,... | collective-permute-start | bytes 36872 | tf_op jit(solution)/shard_map/ppermute | solution.py:17
  31.0 1.5 %collective-permute-start.5 = (f32[4,128,1]{2,1,0:T(8,128)S(1)}, f32[4,128,1]{2,1,0:T(8,128)S(1)}, u32[]{:S(2)}, u32[]{:S(2)}) collective-permute-start(f32[4,128,1]{2,1,0:T(8,128)S(1)} %slice.196), channel_id=1, source_target_pairs={{0,1},{2,3},{4,5},{6,7},{8,9},{10,11},{12,13},{14,15},{16,17},{18,... | collective-permute-start | bytes 6152 | tf_op jit(solution)/shard_map/ppermute | solution.py:17
  40.6 1.4 %collective-permute-done.8 = f32[4,128,1]{2,1,0:T(8,128)S(1)} collective-permute-done((f32[4,128,1]{2,1,0:T(8,128)S(1)}, f32[4,128,1]{2,1,0:T(8,128)S(1)}, u32[]{:S(2)}, u32[]{:S(2)}) %collective-permute-start.8) | collective-permute-done | bytes 2080 | tf_op jit(solution)/shard_map/ppermute | solution.py:17
  42.8 6.0 %collective-permute-done.6 = f32[1,128,768]{2,1,0:T(8,128)S(1)} collective-permute-done((f32[1,128,768]{2,1,0:T(8,128)S(1)}, f32[1,128,768]{2,1,0:T(8,128)S(1)}, u32[]{:S(2)}, u32[]{:S(2)}) %collective-permute-start.6) | collective-permute-done | bytes 393248 | tf_op jit(solution)/shard_map/ppermute | solution.py:17
  48.9 2.1 %fusion.62 = (f32[4,128,768]{2,1,0:T(8,128)S(1)}, f32[4,128,768]{2,1,0:T(8,128)S(1)}, f32[4,128,768]{2,1,0:T(8,128)S(1)}, f32[4,128,768]{2,1,0:T(8,128)S(1)}) fusion(f32[4,128,768]{2,1,0:T(8,128)S(1)} %get-tuple-element.32, f32[128]{0:T(128)S(1)} %and_convert_fusion, f32[4,128,768]{2,1,0:T(8,128)S(1)} %get-tuple-element.21, ...), kind=kLoop, calls=%fused_computation.98 | loop fusion | flops 9437184 | bytes 17305104 | tf_op jit(solution)/shard_map/mul | solution.py:35
  51.8 3.7 %collective-permute-start.9 = (f32[1,128,768]{2,1,0:T(8,128)S(1)}, f32[1,128,768]{2,1,0:T(8,128)S(1)}, u32[]{:S(2)}, u32[]{:S(2)}) collective-permute-start(f32[1,128,768]{2,1,0:T(8,128)S(1)} %slice.204), channel_id=1, source_target_pairs={{0,4},{4,8},{8,12},{1,5},{5,9},{9,13},{2,6},{6,10},{10,14},{3,7},{... | collective-permute-start | bytes 1179656 | tf_op jit(solution)/shard_map/ppermute | solution.py:17
  55.5 4.5 %collective-permute-start.10 = (f32[4,1,768]{2,1,0:T(1,128)S(1)}, f32[4,1,768]{2,1,0:T(1,128)S(1)}, u32[]{:S(2)}, u32[]{:S(2)}) collective-permute-start(f32[4,1,768]{2,1,0:T(1,128)S(1)} %slice.206), channel_id=1, source_target_pairs={{0,2},{1,3},{4,6},{5,7},{8,10},{9,11},{12,14},{13,15},{16,18},{17,... | collective-permute-start | bytes 36872 | tf_op jit(solution)/shard_map/ppermute | solution.py:17
  66.6 1.5 %collective-permute-start.14 = (f32[4,128,1]{2,1,0:T(8,128)S(1)}, f32[4,128,1]{2,1,0:T(8,128)S(1)}, u32[]{:S(2)}, u32[]{:S(2)}) collective-permute-start(f32[4,128,1]{2,1,0:T(8,128)S(1)} %slice.215), channel_id=1, source_target_pairs={{1,0},{3,2},{5,4},{7,6},{9,8},{11,10},{13,12},{15,14},{17,16},{19,... | collective-permute-start | bytes 6152 | tf_op jit(solution)/shard_map/ppermute | solution.py:17
  70.8 6.4 %collective-permute-done.12 = f32[1,128,768]{2,1,0:T(8,128)S(1)} collective-permute-done((f32[1,128,768]{2,1,0:T(8,128)S(1)}, f32[1,128,768]{2,1,0:T(8,128)S(1)}, u32[]{:S(2)}, u32[]{:S(2)}) %collective-permute-start.12) | collective-permute-done | bytes 393248 | tf_op jit(solution)/shard_map/ppermute | solution.py:17
  77.2 2.1 %fusion.65 = (f32[4,128,768]{2,1,0:T(8,128)S(1)}, f32[4,128,768]{2,1,0:T(8,128)S(1)}, f32[4,128,768]{2,1,0:T(8,128)S(1)}, f32[4,128,768]{2,1,0:T(8,128)S(1)}) fusion(f32[4,128,768]{2,1,0:T(8,128)S(1)} %get-tuple-element.30, f32[128]{0:T(128)S(1)} %and_convert_fusion, f32[4,128,768]{2,1,0:T(8,128)S(1)} %get-tuple-element.15, ...), kind=kLoop, calls=%fused_computation.101 | loop fusion | flops 9437184 | bytes 17305104 | tf_op jit(solution)/shard_map/mul | solution.py:35
  80.2 3.5 %collective-permute-start.15 = (f32[1,128,768]{2,1,0:T(8,128)S(1)}, f32[1,128,768]{2,1,0:T(8,128)S(1)}, u32[]{:S(2)}, u32[]{:S(2)}) collective-permute-start(f32[1,128,768]{2,1,0:T(8,128)S(1)} %slice.216), channel_id=1, source_target_pairs={{0,4},{4,8},{8,12},{1,5},{5,9},{9,13},{2,6},{6,10},{10,14},{3,7},{... | collective-permute-start | bytes 1179656 | tf_op jit(solution)/shard_map/ppermute | solution.py:17
  83.7 2.2 %collective-permute-start.16 = (f32[4,1,768]{2,1,0:T(1,128)S(1)}, f32[4,1,768]{2,1,0:T(1,128)S(1)}, u32[]{:S(2)}, u32[]{:S(2)}) collective-permute-start(f32[4,1,768]{2,1,0:T(1,128)S(1)} %slice.218), channel_id=1, source_target_pairs={{0,2},{1,3},{4,6},{5,7},{8,10},{9,11},{12,14},{13,15},{16,18},{17,... | collective-permute-start | bytes 36872 | tf_op jit(solution)/shard_map/ppermute | solution.py:17
  88.5 2.5 %collective-permute-done.15 = f32[1,128,768]{2,1,0:T(8,128)S(1)} collective-permute-done((f32[1,128,768]{2,1,0:T(8,128)S(1)}, f32[1,128,768]{2,1,0:T(8,128)S(1)}, u32[]{:S(2)}, u32[]{:S(2)}) %collective-permute-start.15) | collective-permute-done | bytes 393248 | tf_op jit(solution)/shard_map/ppermute | solution.py:17
  97.0 1.4 %collective-permute-done.20 = f32[4,128,1]{2,1,0:T(8,128)S(1)} collective-permute-done((f32[4,128,1]{2,1,0:T(8,128)S(1)}, f32[4,128,1]{2,1,0:T(8,128)S(1)}, u32[]{:S(2)}, u32[]{:S(2)}) %collective-permute-start.20) | collective-permute-done | bytes 2080 | tf_op jit(solution)/shard_map/ppermute | solution.py:17
  99.2 4.7 %collective-permute-done.18 = f32[1,128,768]{2,1,0:T(8,128)S(1)} collective-permute-done((f32[1,128,768]{2,1,0:T(8,128)S(1)}, f32[1,128,768]{2,1,0:T(8,128)S(1)}, u32[]{:S(2)}, u32[]{:S(2)}) %collective-permute-start.18) | collective-permute-done | bytes 393248 | tf_op jit(solution)/shard_map/ppermute | solution.py:17
  103.9 2.1 %fusion.68 = (f32[4,128,768]{2,1,0:T(8,128)S(1)}, f32[4,128,768]{2,1,0:T(8,128)S(1)}, f32[4,128,768]{2,1,0:T(8,128)S(1)}, f32[4,128,768]{2,1,0:T(8,128)S(1)}) fusion(f32[4,128,768]{2,1,0:T(8,128)S(1)} %get-tuple-element.28, f32[128]{0:T(128)S(1)} %and_convert_fusion, f32[4,128,768]{2,1,0:T(8,128)S(1)} %get-tuple-element.9, ...), kind=kLoop, calls=%fused_computation.104 | loop fusion | flops 9437184 | bytes 17305104 | tf_op jit(solution)/shard_map/mul | solution.py:35
  106.9 3.7 %collective-permute-start.21 = (f32[1,128,768]{2,1,0:T(8,128)S(1)}, f32[1,128,768]{2,1,0:T(8,128)S(1)}, u32[]{:S(2)}, u32[]{:S(2)}) collective-permute-start(f32[1,128,768]{2,1,0:T(8,128)S(1)} %slice.228), channel_id=1, source_target_pairs={{0,4},{4,8},{8,12},{1,5},{5,9},{9,13},{2,6},{6,10},{10,14},{3,7},{... | collective-permute-start | bytes 1179656 | tf_op jit(solution)/shard_map/ppermute | solution.py:17
  114.5 1.6 %collective-permute-done.21 = f32[1,128,768]{2,1,0:T(8,128)S(1)} collective-permute-done((f32[1,128,768]{2,1,0:T(8,128)S(1)}, f32[1,128,768]{2,1,0:T(8,128)S(1)}, u32[]{:S(2)}, u32[]{:S(2)}) %collective-permute-start.21) | collective-permute-done | bytes 393248 | tf_op jit(solution)/shard_map/ppermute | solution.py:17
  116.1 2.2 %fusion.53 = f32[4,128,768]{2,1,0:T(8,128)} fusion(f32[4,128,768]{2,1,0:T(8,128)S(1)} %get-tuple-element.26, f32[3,128,768]{2,1,0:T(8,128)S(1)} %slice.229, f32[1,128,768]{2,1,0:T(8,128)S(1)} %collective-permute-done.21, f32[4,128,768]{2,1,0:T(8,128)S(1)} %get-tuple-element.25, f32[4,127,768]{2,1,0:T(8,128)S(1)} %bitcast.15, ...), kind=kLoop, calls=%fused_computation.75 | loop fusion | flops 5505024 | bytes 14155776 | tf_op jit(solution)/shard_map/div | solution.py:39
  (83 shorter events, 41.4 us)
Async XLA Ops:
  0.9 8.9 %collective-permute-start.1 = (f32[4,1,768]{2,1,0:T(1,128)S(1)}, f32[4,1,768]{2,1,0:T(1,128)S(1)}, u32[]{:S(2)}, u32[]{:S(2)}) collective-permute-start(f32[4,1,768]{2,1,0:T(1,128)S(1)} %slice.147), channel_id=1, source_target_pairs={{2,0},{3,1},{6,4},{7,5},{10,8},{11,9},{14,12},{15,13},{18,16},{19,... | collective-permute-start | bytes 36872 | tf_op jit(solution)/shard_map/ppermute | solution.py:17
  3.2 6.6 %collective-permute-start.2 = (f32[4,128,1]{2,1,0:T(8,128)S(1)}, f32[4,128,1]{2,1,0:T(8,128)S(1)}, u32[]{:S(2)}, u32[]{:S(2)}) collective-permute-start(f32[4,128,1]{2,1,0:T(8,128)S(1)} %slice.149), channel_id=1, source_target_pairs={{1,0},{3,2},{5,4},{7,6},{9,8},{11,10},{13,12},{15,14},{17,16},{19,... | collective-permute-start | bytes 6152 | tf_op jit(solution)/shard_map/ppermute | solution.py:17
  5.6 14.5 %collective-permute-start = (f32[1,128,768]{2,1,0:T(8,128)S(1)}, f32[1,128,768]{2,1,0:T(8,128)S(1)}, u32[]{:S(2)}, u32[]{:S(2)}) collective-permute-start(f32[1,128,768]{2,1,0:T(8,128)S(1)} %slice.145), channel_id=1, source_target_pairs={{4,0},{8,4},{12,8},{5,1},{9,5},{13,9},{6,2},{10,6},{14,10},{7,3},{... | collective-permute-start | bytes 1179656 | tf_op jit(solution)/shard_map/ppermute | solution.py:17
  22.1 12.8 %collective-permute-start.3 = (f32[1,128,768]{2,1,0:T(8,128)S(1)}, f32[1,128,768]{2,1,0:T(8,128)S(1)}, u32[]{:S(2)}, u32[]{:S(2)}) collective-permute-start(f32[1,128,768]{2,1,0:T(8,128)S(1)} %slice.192), channel_id=1, source_target_pairs={{0,4},{4,8},{8,12},{1,5},{5,9},{9,13},{2,6},{6,10},{10,14},{3,7},{... | collective-permute-start | bytes 1179656 | tf_op jit(solution)/shard_map/ppermute | solution.py:17
  26.3 7.3 %collective-permute-start.4 = (f32[4,1,768]{2,1,0:T(1,128)S(1)}, f32[4,1,768]{2,1,0:T(1,128)S(1)}, u32[]{:S(2)}, u32[]{:S(2)}) collective-permute-start(f32[4,1,768]{2,1,0:T(1,128)S(1)} %slice.194), channel_id=1, source_target_pairs={{0,2},{1,3},{4,6},{5,7},{8,10},{9,11},{12,14},{13,15},{16,18},{17,... | collective-permute-start | bytes 36872 | tf_op jit(solution)/shard_map/ppermute | solution.py:17
  31.0 2.6 %collective-permute-start.5 = (f32[4,128,1]{2,1,0:T(8,128)S(1)}, f32[4,128,1]{2,1,0:T(8,128)S(1)}, u32[]{:S(2)}, u32[]{:S(2)}) collective-permute-start(f32[4,128,1]{2,1,0:T(8,128)S(1)} %slice.196), channel_id=1, source_target_pairs={{0,1},{2,3},{4,5},{6,7},{8,9},{10,11},{12,13},{14,15},{16,17},{18,... | collective-permute-start | bytes 6152 | tf_op jit(solution)/shard_map/ppermute | solution.py:17
  35.9 12.9 %collective-permute-start.6 = (f32[1,128,768]{2,1,0:T(8,128)S(1)}, f32[1,128,768]{2,1,0:T(8,128)S(1)}, u32[]{:S(2)}, u32[]{:S(2)}) collective-permute-start(f32[1,128,768]{2,1,0:T(8,128)S(1)} %slice.199), channel_id=1, source_target_pairs={{4,0},{8,4},{12,8},{5,1},{9,5},{13,9},{6,2},{10,6},{14,10},{7,3},{... | collective-permute-start | bytes 1179656 | tf_op jit(solution)/shard_map/ppermute | solution.py:17
  37.2 5.6 %collective-permute-start.7 = (f32[4,1,768]{2,1,0:T(1,128)S(1)}, f32[4,1,768]{2,1,0:T(1,128)S(1)}, u32[]{:S(2)}, u32[]{:S(2)}) collective-permute-start(f32[4,1,768]{2,1,0:T(1,128)S(1)} %slice.201), channel_id=1, source_target_pairs={{2,0},{3,1},{6,4},{7,5},{10,8},{11,9},{14,12},{15,13},{18,16},{19,... | collective-permute-start | bytes 36872 | tf_op jit(solution)/shard_map/ppermute | solution.py:17
  38.6 3.4 %collective-permute-start.8 = (f32[4,128,1]{2,1,0:T(8,128)S(1)}, f32[4,128,1]{2,1,0:T(8,128)S(1)}, u32[]{:S(2)}, u32[]{:S(2)}) collective-permute-start(f32[4,128,1]{2,1,0:T(8,128)S(1)} %slice.203), channel_id=1, source_target_pairs={{1,0},{3,2},{5,4},{7,6},{9,8},{11,10},{13,12},{15,14},{17,16},{19,... | collective-permute-start | bytes 6152 | tf_op jit(solution)/shard_map/ppermute | solution.py:17
  51.8 10.8 %collective-permute-start.9 = (f32[1,128,768]{2,1,0:T(8,128)S(1)}, f32[1,128,768]{2,1,0:T(8,128)S(1)}, u32[]{:S(2)}, u32[]{:S(2)}) collective-permute-start(f32[1,128,768]{2,1,0:T(8,128)S(1)} %slice.204), channel_id=1, source_target_pairs={{0,4},{4,8},{8,12},{1,5},{5,9},{9,13},{2,6},{6,10},{10,14},{3,7},{... | collective-permute-start | bytes 1179656 | tf_op jit(solution)/shard_map/ppermute | solution.py:17
  55.5 7.1 %collective-permute-start.10 = (f32[4,1,768]{2,1,0:T(1,128)S(1)}, f32[4,1,768]{2,1,0:T(1,128)S(1)}, u32[]{:S(2)}, u32[]{:S(2)}) collective-permute-start(f32[4,1,768]{2,1,0:T(1,128)S(1)} %slice.206), channel_id=1, source_target_pairs={{0,2},{1,3},{4,6},{5,7},{8,10},{9,11},{12,14},{13,15},{16,18},{17,... | collective-permute-start | bytes 36872 | tf_op jit(solution)/shard_map/ppermute | solution.py:17
  60.2 2.4 %collective-permute-start.11 = (f32[4,128,1]{2,1,0:T(8,128)S(1)}, f32[4,128,1]{2,1,0:T(8,128)S(1)}, u32[]{:S(2)}, u32[]{:S(2)}) collective-permute-start(f32[4,128,1]{2,1,0:T(8,128)S(1)} %slice.208), channel_id=1, source_target_pairs={{0,1},{2,3},{4,5},{6,7},{8,9},{10,11},{12,13},{14,15},{16,17},{18,... | collective-permute-start | bytes 6152 | tf_op jit(solution)/shard_map/ppermute | solution.py:17
  63.9 13.3 %collective-permute-start.12 = (f32[1,128,768]{2,1,0:T(8,128)S(1)}, f32[1,128,768]{2,1,0:T(8,128)S(1)}, u32[]{:S(2)}, u32[]{:S(2)}) collective-permute-start(f32[1,128,768]{2,1,0:T(8,128)S(1)} %slice.211), channel_id=1, source_target_pairs={{4,0},{8,4},{12,8},{5,1},{9,5},{13,9},{6,2},{10,6},{14,10},{7,3},{... | collective-permute-start | bytes 1179656 | tf_op jit(solution)/shard_map/ppermute | solution.py:17
  65.2 5.6 %collective-permute-start.13 = (f32[4,1,768]{2,1,0:T(1,128)S(1)}, f32[4,1,768]{2,1,0:T(1,128)S(1)}, u32[]{:S(2)}, u32[]{:S(2)}) collective-permute-start(f32[4,1,768]{2,1,0:T(1,128)S(1)} %slice.213), channel_id=1, source_target_pairs={{2,0},{3,1},{6,4},{7,5},{10,8},{11,9},{14,12},{15,13},{18,16},{19,... | collective-permute-start | bytes 36872 | tf_op jit(solution)/shard_map/ppermute | solution.py:17
  66.6 3.4 %collective-permute-start.14 = (f32[4,128,1]{2,1,0:T(8,128)S(1)}, f32[4,128,1]{2,1,0:T(8,128)S(1)}, u32[]{:S(2)}, u32[]{:S(2)}) collective-permute-start(f32[4,128,1]{2,1,0:T(8,128)S(1)} %slice.215), channel_id=1, source_target_pairs={{1,0},{3,2},{5,4},{7,6},{9,8},{11,10},{13,12},{15,14},{17,16},{19,... | collective-permute-start | bytes 6152 | tf_op jit(solution)/shard_map/ppermute | solution.py:17
  80.2 10.9 %collective-permute-start.15 = (f32[1,128,768]{2,1,0:T(8,128)S(1)}, f32[1,128,768]{2,1,0:T(8,128)S(1)}, u32[]{:S(2)}, u32[]{:S(2)}) collective-permute-start(f32[1,128,768]{2,1,0:T(8,128)S(1)} %slice.216), channel_id=1, source_target_pairs={{0,4},{4,8},{8,12},{1,5},{5,9},{9,13},{2,6},{6,10},{10,14},{3,7},{... | collective-permute-start | bytes 1179656 | tf_op jit(solution)/shard_map/ppermute | solution.py:17
  83.7 4.8 %collective-permute-start.16 = (f32[4,1,768]{2,1,0:T(1,128)S(1)}, f32[4,1,768]{2,1,0:T(1,128)S(1)}, u32[]{:S(2)}, u32[]{:S(2)}) collective-permute-start(f32[4,1,768]{2,1,0:T(1,128)S(1)} %slice.218), channel_id=1, source_target_pairs={{0,2},{1,3},{4,6},{5,7},{8,10},{9,11},{12,14},{13,15},{16,18},{17,... | collective-permute-start | bytes 36872 | tf_op jit(solution)/shard_map/ppermute | solution.py:17
  86.1 2.4 %collective-permute-start.17 = (f32[4,128,1]{2,1,0:T(8,128)S(1)}, f32[4,128,1]{2,1,0:T(8,128)S(1)}, u32[]{:S(2)}, u32[]{:S(2)}) collective-permute-start(f32[4,128,1]{2,1,0:T(8,128)S(1)} %slice.220), channel_id=1, source_target_pairs={{0,1},{2,3},{4,5},{6,7},{8,9},{10,11},{12,13},{14,15},{16,17},{18,... | collective-permute-start | bytes 6152 | tf_op jit(solution)/shard_map/ppermute | solution.py:17
  92.3 11.6 %collective-permute-start.18 = (f32[1,128,768]{2,1,0:T(8,128)S(1)}, f32[1,128,768]{2,1,0:T(8,128)S(1)}, u32[]{:S(2)}, u32[]{:S(2)}) collective-permute-start(f32[1,128,768]{2,1,0:T(8,128)S(1)} %slice.223), channel_id=1, source_target_pairs={{4,0},{8,4},{12,8},{5,1},{9,5},{13,9},{6,2},{10,6},{14,10},{7,3},{... | collective-permute-start | bytes 1179656 | tf_op jit(solution)/shard_map/ppermute | solution.py:17
  93.6 5.6 %collective-permute-start.19 = (f32[4,1,768]{2,1,0:T(1,128)S(1)}, f32[4,1,768]{2,1,0:T(1,128)S(1)}, u32[]{:S(2)}, u32[]{:S(2)}) collective-permute-start(f32[4,1,768]{2,1,0:T(1,128)S(1)} %slice.225), channel_id=1, source_target_pairs={{2,0},{3,1},{6,4},{7,5},{10,8},{11,9},{14,12},{15,13},{18,16},{19,... | collective-permute-start | bytes 36872 | tf_op jit(solution)/shard_map/ppermute | solution.py:17
  95.0 3.4 %collective-permute-start.20 = (f32[4,128,1]{2,1,0:T(8,128)S(1)}, f32[4,128,1]{2,1,0:T(8,128)S(1)}, u32[]{:S(2)}, u32[]{:S(2)}) collective-permute-start(f32[4,128,1]{2,1,0:T(8,128)S(1)} %slice.227), channel_id=1, source_target_pairs={{1,0},{3,2},{5,4},{7,6},{9,8},{11,10},{13,12},{15,14},{17,16},{19,... | collective-permute-start | bytes 6152 | tf_op jit(solution)/shard_map/ppermute | solution.py:17
  106.9 9.2 %collective-permute-start.21 = (f32[1,128,768]{2,1,0:T(8,128)S(1)}, f32[1,128,768]{2,1,0:T(8,128)S(1)}, u32[]{:S(2)}, u32[]{:S(2)}) collective-permute-start(f32[1,128,768]{2,1,0:T(8,128)S(1)} %slice.228), channel_id=1, source_target_pairs={{0,4},{4,8},{8,12},{1,5},{5,9},{9,13},{2,6},{6,10},{10,14},{3,7},{... | collective-permute-start | bytes 1179656 | tf_op jit(solution)/shard_map/ppermute | solution.py:17
  110.6 3.9 %collective-permute-start.22 = (f32[4,1,768]{2,1,0:T(1,128)S(1)}, f32[4,1,768]{2,1,0:T(1,128)S(1)}, u32[]{:S(2)}, u32[]{:S(2)}) collective-permute-start(f32[4,1,768]{2,1,0:T(1,128)S(1)} %slice.230), channel_id=1, source_target_pairs={{0,2},{1,3},{4,6},{5,7},{8,10},{9,11},{12,14},{13,15},{16,18},{17,... | collective-permute-start | bytes 36872 | tf_op jit(solution)/shard_map/ppermute | solution.py:17
  112.0 2.4 %collective-permute-start.23 = (f32[4,128,1]{2,1,0:T(8,128)S(1)}, f32[4,128,1]{2,1,0:T(8,128)S(1)}, u32[]{:S(2)}, u32[]{:S(2)}) collective-permute-start(f32[4,128,1]{2,1,0:T(8,128)S(1)} %slice.232), channel_id=1, source_target_pairs={{0,1},{2,3},{4,5},{6,7},{8,9},{10,11},{12,13},{14,15},{16,17},{18,... | collective-permute-start | bytes 6152 | tf_op jit(solution)/shard_map/ppermute | solution.py:17
  (1 other events, 6.0 us)
where the time goes:
time: 119 us; the launch traced here: 118 us
  starting transfers between devices  48.8 us (41%)
  waiting for transfers between devices  43.6 us (37%)
  other arithmetic  17.3 us (15%)
  local copies, waits for them, and re-layouts  8.1 us (7%)
    ppermute x24, starting transfers between devices, from_behind(): lax.ppermute(value, axis, [(source, source + steps) for source in range(i...  48.8 us
    ppermute x24, waiting for transfers between devices, from_behind(): lax.ppermute(value, axis, [(source, source + steps) for source in range(i...  43.6 us
    mul x8, other arithmetic, project(): return (stepped[0] * shrink, stepped[1] * shrink, stepped[2] * shrink)  10.8 us
    sub x3, other arithmetic, body(): relaxed = 2.0 * updated - current  3.39 us
  transfers between devices with their start and end apart: 24, of which 17 were waited for; matrix products, arithmetic and copies ran while one was open for 7% of the time, Pallas kernels for 0%

commit v1 on v0

v1 whole, which is shorter than its diff:
```python
import functools

import jax
import jax.numpy as jnp
from jax import lax
from jax.experimental import pallas as pl
from jax.experimental.pallas import tpu as pltpu
from jax.sharding import PartitionSpec as P

MESH = pl.DeviceIdType.MESH

dual_step = 12.0 ** (-0.5)
primal_step = 12.0 ** (-0.5)
radius = 0.6

reach = radius / dual_step
keep = 1.0 / (1.0 + primal_step)
push = primal_step * dual_step / (1.0 + primal_step)
pull = primal_step / (1.0 + primal_step)

TILE = 8
LANES = 128


def kernel(tm_size, row_size, x, cuts, out, noisy, relaxed, far, current, dual_t, dual_h, dual_w,
           mask_w, load_sem, z_send, z_recv, r_send, r_recv, c_send, c_recv, out_sem):
    frames, rows, cols = x.shape
    high = rows + 2 * TILE
    wide = cols + LANES
    tiles = high // TILE
    tm = lax.axis_index("tm")
    band = lax.axis_index("rows")
    core = lax.axis_index("cols")
    has_left = tm > 0
    has_right = tm < tm_size - 1
    up = lax.rem(band + row_size - 1, row_size)
    down = lax.rem(band + 1, row_size)
    other = 1 - core
    own_rows = pl.ds(TILE, rows)
    own_cols = pl.ds(0, cols)

    def far_slot(level, side):
        return 2 * (level - 1) + side

    def at(level, t):
        if level == 0:
            return noisy.at[t + 2]
        if -1 <= t <= frames:
            return relaxed.at[level - 1, t + 1]
        return far.at[far_slot(level, 0 if t < 0 else 1)]

    def greet(device):
        pl.semaphore_signal(barrier, inc=1, device_id=device, device_id_type=MESH)

    barrier = pltpu.get_barrier_semaphore()
    greet({"rows": up})
    greet({"rows": down})
    greet({"cols": other})

    @pl.when(has_left)
    def _():
        greet({"tm": tm - 1})

    @pl.when(has_right)
    def _():
        greet({"tm": tm + 1})

    load = pltpu.make_async_copy(x, noisy.at[pl.ds(2, frames), own_rows, own_cols], load_sem)
    load.start()
    pl.semaphore_wait(barrier, 3 + has_left.astype(jnp.int32) + has_right.astype(jnp.int32))

    def along_tm(stage):
        if stage == 0:
            ends = (x.at[0], at(0, frames)), (x.at[frames - 1], at(0, -1))
        elif stage == 1:
            ends = (x.at[1], at(0, frames + 1)), (x.at[frames - 2], at(0, -2))
        else:
            level = stage - 1
            ends = (
                (at(level, 1).at[own_rows, own_cols], at(level, frames + 1)),
                (at(level, frames - 2).at[own_rows, own_cols], at(level, -2)),
            )
        return [
            pltpu.make_async_remote_copy(
                src_ref=source,
                dst_ref=target.at[own_rows, own_cols],
                send_sem=z_send.at[stage, side],
                recv_sem=z_recv.at[stage, side],
                device_id={"tm": tm - 1 if side == 0 else tm + 1},
                device_id_type=MESH,
            )
            for side, (source, target) in enumerate(ends)
        ]

    def send_frames(stage):
        left, right = along_tm(stage)
        pl.when(has_left)(left.start)
        pl.when(has_right)(right.start)

    def await_frames(stage):
        left, right = along_tm(stage)
        pl.when(has_right)(left.wait_recv)
        pl.when(has_left)(right.wait_recv)

    def await_sent(stage):
        left, right = along_tm(stage)
        pl.when(has_left)(left.wait_send)
        pl.when(has_right)(right.wait_send)

    def arrived(stage):
        if stage == 0:
            return at(0, frames), at(0, -1)
        if stage == 1:
            return at(0, frames + 1), at(0, -2)
        return at(stage - 1, frames + 1), at(stage - 1, -2)

    def row_halo(slot, source, target):
        first, last = source
        return [
            pltpu.make_async_remote_copy(
                src_ref=first, dst_ref=target[1], send_sem=r_send.at[slot, 0], recv_sem=r_recv.at[slot, 0],
                device_id={"rows": up}, device_id_type=MESH),
            pltpu.make_async_remote_copy(
                src_ref=last, dst_ref=target[0], send_sem=r_send.at[slot, 1], recv_sem=r_recv.at[slot, 1],
                device_id={"rows": down}, device_id_type=MESH),
        ]

    edge = pl.ds(pl.multiple_of(other * (cols - LANES), LANES), LANES)

    def col_halo(slot, source, target):
        return pltpu.make_async_remote_copy(
            src_ref=source, dst_ref=target, send_sem=c_send.at[slot], recv_sem=c_recv.at[slot],
            device_id={"cols": other}, device_id_type=MESH)

    above, below = pl.ds(0, TILE), pl.ds(TILE + rows, TILE)
    all_rows, beyond = pl.ds(0, high), pl.ds(cols, LANES)
    own = pl.ds(2, frames)
    own_row_halo = row_halo(
        0,
        (x.at[:, pl.ds(0, TILE)], x.at[:, pl.ds(rows - TILE, TILE)]),
        (noisy.at[own, above, own_cols], noisy.at[own, below, own_cols]),
    )
    own_col_halo = col_halo(0, noisy.at[own, all_rows, edge], noisy.at[own, all_rows, beyond])

    def row_halos(stage):
        copies = []
        for side, frame in enumerate(arrived(stage)):
            copies += row_halo(
                1 + 2 * stage + side,
                (frame.at[pl.ds(TILE, TILE), own_cols], frame.at[pl.ds(rows, TILE), own_cols]),
                (frame.at[above, own_cols], frame.at[below, own_cols]),
            )
        return copies

    def col_halos(stage):
        return [
            col_halo(1 + 2 * stage + side, frame.at[all_rows, edge], frame.at[all_rows, beyond])
            for side, frame in enumerate(arrived(stage))
        ]

    sub = lax.broadcasted_iota(jnp.int32, (TILE, LANES), 0)
    spread = lambda v: jnp.concatenate([v] * (wide // LANES), axis=1)
    first_row = spread(sub) == 0
    last_row = spread(sub) == TILE - 1
    above_open = band > 0
    below_open = band < row_size - 1

    total_frames = frames * tm_size

    def frame_mask(t):
        g = tm * frames + t
        open_ = (g >= 0) & (g <= total_frames - 2)
        for j in range(cuts.shape[0]):
            open_ = open_ & (cuts[j] != g + 1)
        return jnp.where(open_, 1.0, 0.0).astype(jnp.float32)

    def dual(level, t):
        here, after = at(level - 1, t), at(level - 1, t + 1)
        mask_t = frame_mask(t)

        def step(i, _):
            r = pl.ds(pl.multiple_of(i * TILE, TILE), TILE)
            n = pl.ds(pl.multiple_of(jnp.minimum(i + 1, tiles - 1) * TILE, TILE), TILE)
            v = here[r, :]
            row = sub + i * TILE
            shut = ((row == TILE - 1) & jnp.logical_not(above_open)) | (
                (row == TILE + rows - 1) & jnp.logical_not(below_open))
            mask_h = spread(jnp.where(shut, 0.0, 1.0).astype(jnp.float32))
            a = (after[r, :] - v) * mask_t
            b = (pltpu.roll(jnp.where(first_row, here[n, :], v), TILE - 1, 0) - v) * mask_h
            c = (pltpu.roll(v, wide - 1, 1) - v) * mask_w[...]
            if level > 1:
                a = a + dual_t[t + 2, r, :]
                b = b + dual_h[t + 2, r, :]
                c = c + dual_w[t + 2, r, :]
            shrink = jnp.minimum(1.0, reach * lax.rsqrt(a * a + b * b + c * c))
            dual_t[t + 2, r, :] = a * shrink
            dual_h[t + 2, r, :] = b * shrink
            dual_w[t + 2, r, :] = c * shrink
            return 0

        lax.fori_loop(0, tiles, step, 0)

    def primal(level, t):
        held = current.at[t + 1]
        before = noisy.at[t + 2] if level == 1 else held
        start = noisy.at[t + 2]

        def step(i, _):
            r = pl.ds(pl.multiple_of(i * TILE, TILE), TILE)
            p = pl.ds(pl.multiple_of(jnp.maximum(i - 1, 0) * TILE, TILE), TILE)
            h = dual_h[t + 2, r, :]
            w = dual_w[t + 2, r, :]
            gone = dual_t[t + 2, r, :] - dual_t[t + 1, r, :]
            gone = gone + (h - pltpu.roll(jnp.where(last_row, dual_h[t + 2, p, :], h), 1, 0))
            gone = gone + (w - pltpu.roll(w, 1, 1))
            old = before[r, :]
            new = keep * old + push * gone + pull * start[r, :]
            held[r, :] = new
            if level < 4:
                at(level, t)[r, :] = 2.0 * new - old
            return 0

        lax.fori_loop(0, tiles, step, 0)

    def finish(t):
        return pltpu.make_async_copy(current.at[t + 1, own_rows, own_cols], out.at[t], out_sem.at[t])

    for copy in own_row_halo:
        copy.start()
    send_frames(0)
    lane = lax.broadcasted_iota(jnp.int32, (TILE, wide), 1)
    mask_w[...] = jnp.where(lane == jnp.where(core == 0, wide - 1, cols - 1), 0.0, 1.0).astype(jnp.float32)

    def clear(refs):
        def step(i, _):
            r = pl.ds(pl.multiple_of(i * TILE, TILE), TILE)
            for ref in refs:
                ref[r, :] = jnp.zeros((TILE, wide), jnp.float32)
            return 0

        lax.fori_loop(1, tiles - 1, step, 0)

    @pl.when(jnp.logical_not(has_left))
    def _():
        clear([at(0, -1), at(0, -2), at(1, -2), at(2, -2)])

    @pl.when(jnp.logical_not(has_right))
    def _():
        clear([at(0, frames), at(0, frames + 1), at(1, frames + 1), at(2, frames + 1)])

    load.wait()
    for copy in own_row_halo:
        copy.wait_recv()
    own_col_halo.start()
    own_col_halo.wait_recv()

    def receive(stage):
        await_frames(stage)
        rows_in = row_halos(stage)
        for copy in rows_in:
            copy.start()
        if stage == 0:
            send_frames(1)
        for copy in rows_in:
            copy.wait_recv()
        cols_in = col_halos(stage)
        for copy in cols_in:
            copy.start()
        for copy in cols_in:
            copy.wait_recv()

    dual(1, 0)
    dual(1, 1)
    primal(1, 1)
    dual(1, 2)
    primal(1, 2)
    dual(2, 1)
    receive(0)

    dual(1, -1)
    primal(1, 0)
    dual(1, 3)
    primal(1, 3)
    dual(2, 0)
    primal(2, 1)
    dual(2, 2)
    primal(2, 2)
    send_frames(2)
    dual(3, 1)
    receive(1)

    dual(1, -2)
    primal(1, -1)
    dual(1, 4)
    primal(1, 4)
    dual(2, -1)
    primal(2, 0)
    dual(2, 3)
    primal(2, 3)
    send_frames(3)
    dual(3, 0)
    primal(3, 1)
    dual(3, 2)
    primal(3, 2)
    dual(4, 1)
    receive(2)

    dual(2, -2)
    primal(2, -1)
    dual(2, 4)
    primal(2, 4)
    dual(3, -1)
    primal(3, 0)
    dual(3, 3)
    primal(3, 3)
    dual(4, 0)
    primal(4, 1)
    finish(1).start()
    dual(4, 2)
    primal(4, 2)
    finish(2).start()
    receive(3)

    dual(3, -2)
    primal(3, -1)
    dual(4, -1)
    primal(4, 0)
    finish(0).start()
    dual(3, 4)
    primal(3, 4)
    dual(4, 3)
    primal(4, 3)
    finish(3).start()

    for stage in range(4):
        await_sent(stage)
        for copy in row_halos(stage) + col_halos(stage):
            copy.wait_send()
    for copy in own_row_halo + [own_col_halo]:
        copy.wait_send()
    for t in range(frames):
        finish(t).wait()


def solution(mesh):
    tm_size, row_size = mesh.shape["tm"], mesh.shape["rows"]

    def body(noisy_luma, scene_cuts):
        frames, rows, cols = noisy_luma.shape
        field = (rows + 2 * TILE, cols + LANES)
        buffer = lambda *lead: pltpu.VMEM(lead + field, jnp.float32)
        dma = pltpu.SemaphoreType.DMA
        return pl.pallas_call(
            functools.partial(kernel, tm_size, row_size),
            out_shape=jax.ShapeDtypeStruct(noisy_luma.shape, jnp.float32),
            in_specs=[pl.BlockSpec(memory_space=pl.ANY), pl.BlockSpec(memory_space=pltpu.SMEM)],
            out_specs=pl.BlockSpec(memory_space=pl.ANY),
            scratch_shapes=[
                buffer(frames + 4),
                buffer(3, frames + 2),
                buffer(4),
                buffer(frames + 2),
                buffer(frames + 3),
                buffer(frames + 3),
                buffer(frames + 3),
                pltpu.VMEM((TILE, cols + LANES), jnp.float32),
                dma(()),
                dma((4, 2)),
                dma((4, 2)),
                dma((9, 2)),
                dma((9, 2)),
                dma((9,)),
                dma((9,)),
                dma((frames,)),
            ],
            compiler_params=pltpu.CompilerParams(
                collective_id=0, has_side_effects=True, vmem_limit_bytes=48 * 1024 * 1024),
        )(noisy_luma, scene_cuts)

    return jax.shard_map(
        body,
        mesh=mesh,
        in_specs=(P(("film", "tm"), "rows", "cols"), P("film")),
        out_specs=P(("film", "tm"), "rows", "cols"),
        check_vma=False,
    )
```

time: 119 us -> 112 us (0.941)
  Pallas kernels: 0 us -> 108 us
  starting transfers between devices: 48.8 us -> 0 us
  waiting for transfers between devices: 43.6 us -> 0 us
  other arithmetic: 17.3 us -> 0 us
  local copies, waits for them, and re-layouts: 8.1 us -> 3.21 us
    pallas_call x0 -> x1, Pallas kernels: none -> 108 us  [body(): pl.pallas_call(functools.partial(kernel, tm_size, row_size), out_shape=ja...]
    ppermute x24 -> x0, starting transfers between devices: 48.8 us -> none  [from_behind(): lax.ppermute(value, axis, [(source, source + steps) for source in range(i...]
    ppermute x24 -> x0, waiting for transfers between devices: 43.6 us -> none  [from_behind(): lax.ppermute(value, axis, [(source, source + steps) for source in range(i...]
    mul x8 -> x0, other arithmetic: 10.8 us -> none  [project(): return (stepped[0] * shrink, stepped[1] * shrink, stepped[2] * shrink)]
    slice x40 -> x0, local copies, waits for them, and re-layouts: 8.09 us -> none  [the longest x4 1.88 us: forward_faces(): values[:, :, 1:]]
    sub x3 -> x0, other arithmetic: 3.39 us -> none  [body(): relaxed = 2.0 * updated - current]
    unnamed x2 -> x5, local copies, waits for them, and re-layouts: 0.01 us -> 3.21 us
    div x1 -> x0, other arithmetic: 2.21 us -> none  [primal_update(): (current + primal_step * diverged + primal_step * noisy_luma) / (1.0 + pr...]
  transfers between devices with their start and end apart: 24 -> 0, of which waited for: 17 -> 0; matrix products, arithmetic and copies ran while one was open for 7% -> 0% of each run, Pallas kernels for 0% -> 0%
where the time goes in v1:
time: 112 us; the launch traced here: 111 us
  Pallas kernels  108 us (96%)
  local copies, waits for them, and re-layouts  3.21 us (3%)
    pallas_call x1, Pallas kernels, body(): pl.pallas_call(functools.partial(kernel, tm_size, row_size), out_shape=ja...  108 us
    unnamed x5, local copies, waits for them, and re-layouts  3.21 us

profile of v1, /device:TPU:0, one launch (start us, length us, event | category | flops | bytes accessed | tf_op | source)
XLA Modules:
  0.0 111.2 jit_solution(1250788352011007140)
XLA Ops:
  0.0 0.0 copy-start
  0.0 1.4 %copy-done = f32[4,128,768]{2,1,0:T(8,128)S(1)} copy-done((f32[4,128,768]{2,1,0:T(8,128)S(1)}, f32[4,128,768]{2,1,0:T(8,128)}, u32[]{:S(2)}) %copy-start) | copy-done | bytes 1572888
  1.4 0.0 copy-start.1
  1.4 0.7 copy-done.1
  2.1 108.0 %shard_map.28 = f32[4,128,768]{2,1,0:T(8,128)S(1)} custom-call(f32[4,128,768]{2,1,0:T(8,128)S(1)} %copy-done, s32[3]{0:T(128)S(1)} %copy-done.1), custom_call_target="tpu_custom_call" | custom-call | tf_op jit(solution)/shard_map/pallas_call | solution.py:354
  110.0 1.1 %copy.4 = f32[4,128,768]{2,1,0:T(8,128)} copy(f32[4,128,768]{2,1,0:T(8,128)S(1)} %shard_map.28) | data formatting | bytes 3145728
Async XLA Ops:
  0.0 1.4 %copy-start = (f32[4,128,768]{2,1,0:T(8,128)S(1)}, f32[4,128,768]{2,1,0:T(8,128)}, u32[]{:S(2)}) copy-start(f32[4,128,768]{2,1,0:T(8,128)} %x.1) | copy-start | bytes 4718596
  1.4 0.7 copy-start.1

commit v2 on v1

v2 whole, which is shorter than its diff:
```python
import functools

import jax
import jax.numpy as jnp
from jax import lax
from jax.experimental import pallas as pl
from jax.experimental.pallas import tpu as pltpu
from jax.sharding import PartitionSpec as P

MESH = pl.DeviceIdType.MESH

dual_step = 12.0 ** (-0.5)
primal_step = 12.0 ** (-0.5)
radius = 0.6

reach = radius / dual_step
keep = 1.0 / (1.0 + primal_step)
push = primal_step * dual_step / (1.0 + primal_step)
pull = primal_step / (1.0 + primal_step)

TILE = 8
LANES = 128
DEEP = 4


def kernel(tm_size, row_size, x, cuts, out, noisy, relaxed, far, current, dual_t, dual_h, dual_w,
           mask_h, mask_w, load_sem, z_send, z_recv, h_send, h_recv, out_sem):
    frames, rows, cols = x.shape
    high = rows + TILE
    wide = cols + LANES
    tm = lax.axis_index("tm")
    band = lax.axis_index("rows")
    core = lax.axis_index("cols")
    has_left = tm > 0
    has_right = tm < tm_size - 1
    has_up = band > 0
    has_down = band < row_size - 1
    other = 1 - core
    own_rows = pl.ds(0, rows)
    own_cols = pl.ds(0, cols)

    def at(level, t):
        if level == 0:
            return noisy.at[t + 2]
        if -1 <= t <= frames:
            return relaxed.at[level - 1, t + 1]
        return far.at[2 * (level - 1) + (0 if t < 0 else 1)]

    for ref in (noisy, far):
        for f in range(ref.shape[0]):
            ref[f, rows:high, :] = jnp.zeros((TILE, wide), jnp.float32)

    barrier = pltpu.get_barrier_semaphore()

    def greet(device):
        pl.semaphore_signal(barrier, inc=1, device_id=device, device_id_type=MESH)

    greet({"cols": other})

    @pl.when(has_up)
    def _():
        greet({"rows": band - 1})
        greet({"rows": band - 1, "cols": other})

    @pl.when(has_down)
    def _():
        greet({"rows": band + 1})
        greet({"rows": band + 1, "cols": other})

    @pl.when(has_left)
    def _():
        greet({"tm": tm - 1})

    @pl.when(has_right)
    def _():
        greet({"tm": tm + 1})

    load = pltpu.make_async_copy(x, noisy.at[pl.ds(2, frames), own_rows, own_cols], load_sem)
    load.start()
    count = lambda flag: flag.astype(jnp.int32)
    pl.semaphore_wait(barrier, 1 + 2 * count(has_up) + 2 * count(has_down) + count(has_left) + count(has_right))

    def along_tm(stage):
        if stage == 0:
            ends = (x.at[0], at(0, frames)), (x.at[frames - 1], at(0, -1))
        elif stage == 1:
            ends = (x.at[1], at(0, frames + 1)), (x.at[frames - 2], at(0, -2))
        else:
            level = stage - 1
            ends = (
                (at(level, 1).at[own_rows, own_cols], at(level, frames + 1)),
                (at(level, frames - 2).at[own_rows, own_cols], at(level, -2)),
            )
        return [
            pltpu.make_async_remote_copy(
                src_ref=source,
                dst_ref=target.at[own_rows, own_cols],
                send_sem=z_send.at[stage, side],
                recv_sem=z_recv.at[stage, side],
                device_id={"tm": tm - 1 if side == 0 else tm + 1},
                device_id_type=MESH,
            )
            for side, (source, target) in enumerate(ends)
        ]

    def send_frames(stage):
        left, right = along_tm(stage)
        pl.when(has_left)(left.start)
        pl.when(has_right)(right.start)

    def await_frames(stage):
        left, right = along_tm(stage)
        pl.when(has_right)(left.wait_recv)
        pl.when(has_left)(right.wait_recv)

    def await_sent(stage):
        left, right = along_tm(stage)
        pl.when(has_left)(left.wait_send)
        pl.when(has_right)(right.wait_send)

    edge = pl.ds(pl.multiple_of(other * (cols - LANES), LANES), LANES)
    beyond = pl.ds(cols, LANES)
    below, above = pl.ds(rows, DEEP), pl.ds(rows + DEEP, DEEP)
    first, last = pl.ds(0, DEEP), pl.ds(rows - DEEP, DEEP)

    def halo(slot, source, target, lead=()):
        def copy(n, src, dst, device):
            return pltpu.make_async_remote_copy(
                src_ref=source.at[lead_src + src], dst_ref=target.at[lead + dst],
                send_sem=h_send.at[slot, n], recv_sem=h_recv.at[slot, n],
                device_id=device, device_id_type=MESH)

        lead_src = (slice(None),) if lead else ()
        ups = [
            copy(0, (first, own_cols), (below, own_cols), {"rows": band - 1}),
            copy(1, (first, edge), (below, beyond), {"rows": band - 1, "cols": other}),
        ]
        downs = [
            copy(2, (last, own_cols), (above, own_cols), {"rows": band + 1}),
            copy(3, (last, edge), (above, beyond), {"rows": band + 1, "cols": other}),
        ]
        side = copy(4, (own_rows, edge), (own_rows, beyond), {"cols": other})
        return ups, downs, side

    def halo_start(copies):
        ups, downs, side = copies
        side.start()

        @pl.when(has_up)
        def _():
            for c in ups:
                c.start()

        @pl.when(has_down)
        def _():
            for c in downs:
                c.start()

    def halo_wait_recv(copies):
        ups, downs, side = copies
        side.wait_recv()

        @pl.when(has_down)
        def _():
            for c in ups:
                c.wait_recv()

        @pl.when(has_up)
        def _():
            for c in downs:
                c.wait_recv()

    def halo_wait_send(copies):
        ups, downs, side = copies
        side.wait_send()

        @pl.when(has_up)
        def _():
            for c in ups:
                c.wait_send()

        @pl.when(has_down)
        def _():
            for c in downs:
                c.wait_send()

    own_halo = halo(0, x, noisy, (pl.ds(2, frames),))

    def halos(stage):
        if stage == 0:
            arrived = at(0, frames), at(0, -1)
        elif stage == 1:
            arrived = at(0, frames + 1), at(0, -2)
        else:
            arrived = at(stage - 1, frames + 1), at(stage - 1, -2)
        return [halo(1 + 2 * stage + side, frame, frame) for side, frame in enumerate(arrived)]

    total_frames = frames * tm_size

    def frame_mask(t):
        g = tm * frames + t
        open_ = (g >= 0) & (g <= total_frames - 2)
        for j in range(cuts.shape[0]):
            open_ = open_ & (cuts[j] != g + 1)
        return jnp.where(open_, 1.0, 0.0).astype(jnp.float32)

    frame_masks = {t: frame_mask(t) for t in range(-2, frames + 1)}
    sub = lax.broadcasted_iota(jnp.int32, (TILE, wide), 0)
    first_row = sub == 0
    last_row = sub == TILE - 1

    def dual(level, t):
        here, after = at(level - 1, t), at(level - 1, t + 1)
        for i in range(0, high, TILE):
            r, n = pl.ds(i, TILE), pl.ds((i + TILE) % high, TILE)
            v = here[r, :]
            a = (after[r, :] - v) * frame_masks[t]
            b = pltpu.roll(jnp.where(first_row, here[n, :], v), TILE - 1, 0) - v
            if i >= rows - TILE:
                b = b * mask_h[pl.ds(i - rows + TILE, TILE), :]
            c = (pltpu.roll(v, wide - 1, 1) - v) * mask_w[...]
            if level > 1:
                a = a + dual_t[t + 2, r, :]
                b = b + dual_h[t + 2, r, :]
                c = c + dual_w[t + 2, r, :]
            shrink = jnp.minimum(1.0, reach * lax.rsqrt(a * a + b * b + c * c))
            dual_t[t + 2, r, :] = a * shrink
            dual_h[t + 2, r, :] = b * shrink
            dual_w[t + 2, r, :] = c * shrink

    def primal(level, t):
        held = current.at[t + 1]
        start = noisy.at[t + 2]
        before = start if level == 1 else held
        for i in range(0, rows if level == 4 else high, TILE):
            r, p = pl.ds(i, TILE), pl.ds((i - TILE) % high, TILE)
            h = dual_h[t + 2, r, :]
            w = dual_w[t + 2, r, :]
            gone = dual_t[t + 2, r, :] - dual_t[t + 1, r, :]
            gone = gone + (h - pltpu.roll(jnp.where(last_row, dual_h[t + 2, p, :], h), 1, 0))
            gone = gone + (w - pltpu.roll(w, 1, 1))
            old = before[r, :]
            new = keep * old + push * gone + pull * start[r, :]
            held[r, :] = new
            if level < 4:
                at(level, t)[r, :] = 2.0 * new - old

    def finish(t):
        return pltpu.make_async_copy(current.at[t + 1, own_rows, own_cols], out.at[t], out_sem.at[t])

    send_frames(0)
    halo_start(own_halo)
    lane = lax.broadcasted_iota(jnp.int32, (TILE, wide), 1)
    mask_w[...] = jnp.where(lane == jnp.where(core == 0, wide - 1, cols - 1), 0.0, 1.0).astype(jnp.float32)
    mask_h[0:TILE, :] = jnp.where(last_row & jnp.logical_not(has_down), 0.0, 1.0).astype(jnp.float32)
    mask_h[TILE : 2 * TILE, :] = jnp.where(last_row & jnp.logical_not(has_up), 0.0, 1.0).astype(jnp.float32)

    def clear(refs):
        def step(i, _):
            r = pl.ds(pl.multiple_of(i * TILE, TILE), TILE)
            for ref in refs:
                ref[r, own_cols] = jnp.zeros((TILE, cols), jnp.float32)
            return 0

        lax.fori_loop(0, rows // TILE, step, 0)

    @pl.when(jnp.logical_not(has_left))
    def _():
        clear([at(0, -1), at(0, -2), at(1, -2), at(2, -2)])

    @pl.when(jnp.logical_not(has_right))
    def _():
        clear([at(0, frames), at(0, frames + 1), at(1, frames + 1), at(2, frames + 1)])

    load.wait()
    halo_wait_recv(own_halo)

    def forward(stage):
        await_frames(stage)
        for copies in halos(stage):
            halo_start(copies)

    def receive(stage):
        for copies in halos(stage):
            halo_wait_recv(copies)

    dual(1, 0)
    dual(1, 1)
    primal(1, 1)
    dual(1, 2)
    primal(1, 2)
    forward(0)
    send_frames(1)
    dual(2, 1)
    receive(0)

    dual(1, -1)
    primal(1, 0)
    dual(1, 3)
    primal(1, 3)
    dual(2, 0)
    primal(2, 1)
    dual(2, 2)
    primal(2, 2)
    send_frames(2)
    forward(1)
    dual(3, 1)
    receive(1)

    dual(1, -2)
    primal(1, -1)
    dual(1, 4)
    primal(1, 4)
    dual(2, -1)
    primal(2, 0)
    dual(2, 3)
    primal(2, 3)
    send_frames(3)
    dual(3, 0)
    primal(3, 1)
    dual(3, 2)
    primal(3, 2)
    forward(2)
    dual(4, 1)
    receive(2)

    dual(2, -2)
    primal(2, -1)
    dual(2, 4)
    primal(2, 4)
    dual(3, -1)
    primal(3, 0)
    dual(3, 3)
    primal(3, 3)
    dual(4, 0)
    primal(4, 1)
    finish(1).start()
    forward(3)
    dual(4, 2)
    primal(4, 2)
    finish(2).start()
    receive(3)

    dual(3, -2)
    primal(3, -1)
    dual(4, -1)
    primal(4, 0)
    finish(0).start()
    dual(3, 4)
    primal(3, 4)
    dual(4, 3)
    primal(4, 3)
    finish(3).start()

    for stage in range(4):
        await_sent(stage)
        for copies in halos(stage):
            halo_wait_send(copies)
    halo_wait_send(own_halo)
    for t in range(frames):
        finish(t).wait()


def solution(mesh):
    tm_size, row_size = mesh.shape["tm"], mesh.shape["rows"]

    def body(noisy_luma, scene_cuts):
        frames, rows, cols = noisy_luma.shape
        field = (rows + TILE, cols + LANES)
        buffer = lambda *lead: pltpu.VMEM(lead + field, jnp.float32)
        dma = pltpu.SemaphoreType.DMA
        return pl.pallas_call(
            functools.partial(kernel, tm_size, row_size),
            out_shape=jax.ShapeDtypeStruct(noisy_luma.shape, jnp.float32),
            in_specs=[pl.BlockSpec(memory_space=pl.ANY), pl.BlockSpec(memory_space=pltpu.SMEM)],
            out_specs=pl.BlockSpec(memory_space=pl.ANY),
            scratch_shapes=[
                buffer(frames + 4),
                buffer(3, frames + 2),
                buffer(4),
                buffer(frames + 2),
                buffer(frames + 3),
                buffer(frames + 3),
                buffer(frames + 3),
                pltpu.VMEM((2 * TILE, cols + LANES), jnp.float32),
                pltpu.VMEM((TILE, cols + LANES), jnp.float32),
                dma(()),
                dma((4, 2)),
                dma((4, 2)),
                dma((9, 5)),
                dma((9, 5)),
                dma((frames,)),
            ],
            compiler_params=pltpu.CompilerParams(
                collective_id=0, has_side_effects=True, vmem_limit_bytes=48 * 1024 * 1024),
        )(noisy_luma, scene_cuts)

    return jax.shard_map(
        body,
        mesh=mesh,
        in_specs=(P(("film", "tm"), "rows", "cols"), P("film")),
        out_specs=P(("film", "tm"), "rows", "cols"),
        check_vma=False,
    )
```

time: 112 us -> 52 us (0.46)
  Pallas kernels: 108 us -> 48.6 us
    pallas_call x1, Pallas kernels: 108 us -> 48.6 us  [body(): pl.pallas_call(functools.partial(kernel, tm_size, row_size), out_shape=ja...]
where the time goes in v2:
time: 52 us; the launch traced here: 51.8 us
  Pallas kernels  48.6 us (93%)
  local copies, waits for them, and re-layouts  3.21 us (6%)
    pallas_call x1, Pallas kernels, body(): pl.pallas_call(functools.partial(kernel, tm_size, row_size), out_shape=ja...  48.6 us
    unnamed x5, local copies, waits for them, and re-layouts  3.21 us

profile of v2, /device:TPU:0, one launch (start us, length us, event | category | flops | bytes accessed | tf_op | source)
XLA Modules:
  0.0 51.8 jit_solution(16591060816207373826)
XLA Ops:
  0.0 0.0 copy-start
  0.0 1.4 %copy-done = f32[4,128,768]{2,1,0:T(8,128)S(1)} copy-done((f32[4,128,768]{2,1,0:T(8,128)S(1)}, f32[4,128,768]{2,1,0:T(8,128)}, u32[]{:S(2)}) %copy-start) | copy-done | bytes 1572888
  1.4 0.0 copy-start.1
  1.4 0.7 %copy-done.1 = s32[3]{0:T(128)S(1)} copy-done((s32[3]{0:T(128)S(1)}, s32[3]{0:T(128)}, u32[]{:S(2)}) %copy-start.1) | copy-done | bytes 36
  2.1 48.6 %shard_map.28 = f32[4,128,768]{2,1,0:T(8,128)S(1)} custom-call(f32[4,128,768]{2,1,0:T(8,128)S(1)} %copy-done, s32[3]{0:T(128)S(1)} %copy-done.1), custom_call_target="tpu_custom_call" | custom-call | tf_op jit(solution)/shard_map/pallas_call | solution.py:372
  50.7 1.1 %copy.4 = f32[4,128,768]{2,1,0:T(8,128)} copy(f32[4,128,768]{2,1,0:T(8,128)S(1)} %shard_map.28) | data formatting | bytes 3145728
Async XLA Ops:
  0.0 1.4 %copy-start = (f32[4,128,768]{2,1,0:T(8,128)S(1)}, f32[4,128,768]{2,1,0:T(8,128)}, u32[]{:S(2)}) copy-start(f32[4,128,768]{2,1,0:T(8,128)} %x.1) | copy-start | bytes 4718596
  1.4 0.7 %copy-start.1 = (s32[3]{0:T(128)S(1)}, s32[3]{0:T(128)}, u32[]{:S(2)}) copy-start(s32[3]{0:T(128)} %cuts.1) | copy-start | bytes 40

commit v3 on v2

--- a/solution.py
+++ b/solution.py
@@ -28,6 +28,7 @@
     frames, rows, cols = x.shape
     high = rows + TILE
     wide = cols + LANES
+    split = 3 * (rows // TILE) // 4
     tm = lax.axis_index("tm")
     band = lax.axis_index("rows")
     core = lax.axis_index("cols")
@@ -80,21 +81,25 @@
     count = lambda flag: flag.astype(jnp.int32)
     pl.semaphore_wait(barrier, 1 + 2 * count(has_up) + 2 * count(has_down) + count(has_left) + count(has_right))
 
+    cut = split * TILE
+    parts = {3: pl.ds(0, cut), 4: pl.ds(cut, rows - cut)}
+
     def along_tm(stage):
+        part = parts.get(stage, own_rows)
         if stage == 0:
             ends = (x.at[0], at(0, frames)), (x.at[frames - 1], at(0, -1))
         elif stage == 1:
             ends = (x.at[1], at(0, frames + 1)), (x.at[frames - 2], at(0, -2))
         else:
-            level = stage - 1
+            level = min(stage, 3) - 1
             ends = (
-                (at(level, 1).at[own_rows, own_cols], at(level, frames + 1)),
-                (at(level, frames - 2).at[own_rows, own_cols], at(level, -2)),
+                (at(level, 1).at[part, own_cols], at(level, frames + 1)),
+                (at(level, frames - 2).at[part, own_cols], at(level, -2)),
             )
         return [
             pltpu.make_async_remote_copy(
                 src_ref=source,
-                dst_ref=target.at[own_rows, own_cols],
+                dst_ref=target.at[part, own_cols],
                 send_sem=z_send.at[stage, side],
                 recv_sem=z_recv.at[stage, side],
                 device_id={"tm": tm - 1 if side == 0 else tm + 1},
@@ -123,7 +128,7 @@
     below, above = pl.ds(rows, DEEP), pl.ds(rows + DEEP, DEEP)
     first, last = pl.ds(0, DEEP), pl.ds(rows - DEEP, DEEP)
 
-    def halo(slot, source, target, lead=()):
+    def halo(slot, source, target, lead=(), stage=None):
         def copy(n, src, dst, device):
             return pltpu.make_async_remote_copy(
                 src_ref=source.at[lead_src + src], dst_ref=target.at[lead + dst],
@@ -139,8 +144,9 @@
             copy(2, (last, own_cols), (above, own_cols), {"rows": band + 1}),
             copy(3, (last, edge), (above, beyond), {"rows": band + 1, "cols": other}),
         ]
-        side = copy(4, (own_rows, edge), (own_rows, beyond), {"cols": other})
-        return ups, downs, side
+        part = parts.get(stage, own_rows)
+        side = copy(5 if stage == 4 else 4, (part, edge), (part, beyond), {"cols": other})
+        return [] if stage == 4 else ups, [] if stage == 3 else downs, side
 
     def halo_start(copies):
         ups, downs, side = copies
@@ -192,8 +198,8 @@
         elif stage == 1:
             arrived = at(0, frames + 1), at(0, -2)
         else:
-            arrived = at(stage - 1, frames + 1), at(stage - 1, -2)
-        return [halo(1 + 2 * stage + side, frame, frame) for side, frame in enumerate(arrived)]
+            arrived = at(min(stage, 3) - 1, frames + 1), at(min(stage, 3) - 1, -2)
+        return [halo(1 + 2 * min(stage, 3) + side, frame, frame, (), stage) for side, frame in enumerate(arrived)]
 
     total_frames = frames * tm_size
 
@@ -209,9 +215,11 @@
     first_row = sub == 0
     last_row = sub == TILE - 1
 
-    def dual(level, t):
+    count_own = rows // TILE
+
+    def dual(level, t, tiles=range(count_own + 1)):
         here, after = at(level - 1, t), at(level - 1, t + 1)
-        for i in range(0, high, TILE):
+        for i in (tile * TILE for tile in tiles):
             r, n = pl.ds(i, TILE), pl.ds((i + TILE) % high, TILE)
             v = here[r, :]
             a = (after[r, :] - v) * frame_masks[t]
@@ -228,11 +236,13 @@
             dual_h[t + 2, r, :] = b * shrink
             dual_w[t + 2, r, :] = c * shrink
 
-    def primal(level, t):
+    def primal(level, t, tiles=None):
+        if tiles is None:
+            tiles = range(count_own if level == 4 else count_own + 1)
         held = current.at[t + 1]
         start = noisy.at[t + 2]
         before = start if level == 1 else held
-        for i in range(0, rows if level == 4 else high, TILE):
+        for i in (tile * TILE for tile in tiles):
             r, p = pl.ds(i, TILE), pl.ds((i - TILE) % high, TILE)
             h = dual_h[t + 2, r, :]
             w = dual_w[t + 2, r, :]
@@ -250,6 +260,7 @@
 
     send_frames(0)
     halo_start(own_halo)
+    send_frames(1)
     lane = lax.broadcasted_iota(jnp.int32, (TILE, wide), 1)
     mask_w[...] = jnp.where(lane == jnp.where(core == 0, wide - 1, cols - 1), 0.0, 1.0).astype(jnp.float32)
     mask_h[0:TILE, :] = jnp.where(last_row & jnp.logical_not(has_down), 0.0, 1.0).astype(jnp.float32)
@@ -289,8 +300,8 @@
     primal(1, 1)
     dual(1, 2)
     primal(1, 2)
+    send_frames(2)
     forward(0)
-    send_frames(1)
     dual(2, 1)
     receive(0)
 
@@ -302,7 +313,8 @@
     primal(2, 1)
     dual(2, 2)
     primal(2, 2)
-    send_frames(2)
+    send_frames(3)
+    send_frames(4)
     forward(1)
     dual(3, 1)
     receive(1)
@@ -315,7 +327,6 @@
     primal(2, 0)
     dual(2, 3)
     primal(2, 3)
-    send_frames(3)
     dual(3, 0)
     primal(3, 1)
     dual(3, 2)
@@ -341,18 +352,30 @@
     finish(2).start()
     receive(3)
 
-    dual(3, -2)
-    primal(3, -1)
-    dual(4, -1)
-    primal(4, 0)
-    finish(0).start()
-    dual(3, 4)
-    primal(3, 4)
-    dual(4, 3)
-    primal(4, 3)
-    finish(3).start()
-
-    for stage in range(4):
+    k, n = split, count_own
+    for late in (False, True):
+        if late:
+            forward(4)
+            receive(4)
+            duals, primals = [*range(k - 1, n + 1)], [*range(k - 1, n + 1), 0]
+            last_duals, last_primals = [*range(k - 2, n + 1), 0], [*range(k - 2, n), 0, 1]
+        else:
+            duals, primals = range(k - 1), range(1, k - 1)
+            last_duals, last_primals = range(1, k - 2), range(2, k - 2)
+        dual(3, -2, duals)
+        primal(3, -1, primals)
+        dual(4, -1, last_duals)
+        primal(4, 0, last_primals)
+        if late:
+            finish(0).start()
+        dual(3, 4, duals)
+        primal(3, 4, primals)
+        dual(4, 3, last_duals)
+        primal(4, 3, last_primals)
+        if late:
+            finish(3).start()
+
+    for stage in range(5):
         await_sent(stage)
         for copies in halos(stage):
             halo_wait_send(copies)
@@ -385,10 +408,10 @@
                 pltpu.VMEM((2 * TILE, cols + LANES), jnp.float32),
                 pltpu.VMEM((TILE, cols + LANES), jnp.float32),
                 dma(()),
-                dma((4, 2)),
-                dma((4, 2)),
-                dma((9, 5)),
-                dma((9, 5)),
+                dma((5, 2)),
+                dma((5, 2)),
+                dma((9, 6)),
+                dma((9, 6)),
                 dma((frames,)),
             ],
             compiler_params=pltpu.CompilerParams(

time: 52 us -> 49.9 us (0.960)
  Pallas kernels: 48.6 us -> 46.2 us
    pallas_call x1, Pallas kernels: 48.6 us -> 46.2 us  [body(): pl.pallas_call(functools.partial(kernel, tm_size, row_size), out_shape=ja...]
where the time goes in v3:
time: 49.9 us; the launch traced here: 49.4 us
  Pallas kernels  46.2 us (93%)
  local copies, waits for them, and re-layouts  3.21 us (6%)
    pallas_call x1, Pallas kernels, body(): pl.pallas_call(functools.partial(kernel, tm_size, row_size), out_shape=ja...  46.2 us
    unnamed x5, local copies, waits for them, and re-layouts  3.21 us

profile of v3, /device:TPU:0, one launch (start us, length us, event | category | flops | bytes accessed | tf_op | source)
XLA Modules:
  0.0 49.4 jit_solution(10018507722788108551)
XLA Ops:
  0.0 0.0 copy-start
  0.0 1.4 %copy-done = f32[4,128,768]{2,1,0:T(8,128)S(1)} copy-done((f32[4,128,768]{2,1,0:T(8,128)S(1)}, f32[4,128,768]{2,1,0:T(8,128)}, u32[]{:S(2)}) %copy-start) | copy-done | bytes 1572888
  1.4 0.0 copy-start.1
  1.4 0.7 %copy-done.1 = s32[3]{0:T(128)S(1)} copy-done((s32[3]{0:T(128)S(1)}, s32[3]{0:T(128)}, u32[]{:S(2)}) %copy-start.1) | copy-done | bytes 36
  2.1 46.2 %shard_map.28 = f32[4,128,768]{2,1,0:T(8,128)S(1)} custom-call(f32[4,128,768]{2,1,0:T(8,128)S(1)} %copy-done, s32[3]{0:T(128)S(1)} %copy-done.1), custom_call_target="tpu_custom_call" | custom-call | tf_op jit(solution)/shard_map/pallas_call | solution.py:395
  48.3 1.1 %copy.4 = f32[4,128,768]{2,1,0:T(8,128)} copy(f32[4,128,768]{2,1,0:T(8,128)S(1)} %shard_map.28) | data formatting | bytes 3145728
Async XLA Ops:
  0.0 1.4 %copy-start = (f32[4,128,768]{2,1,0:T(8,128)S(1)}, f32[4,128,768]{2,1,0:T(8,128)}, u32[]{:S(2)}) copy-start(f32[4,128,768]{2,1,0:T(8,128)} %x.1) | copy-start | bytes 4718596
  1.4 0.7 %copy-start.1 = (s32[3]{0:T(128)S(1)}, s32[3]{0:T(128)}, u32[]{:S(2)}) copy-start(s32[3]{0:T(128)} %cuts.1) | copy-start | bytes 40
